TPU v7x, 32 devices: a whole 2x2x4 slice. The times are simulated.
32 devices in a mesh: section: 2 (over x), expert: 16 (over z, y, core).
Axes of the slice: x: 2, y: 2, z: 4, core: 2. Of those that a mesh axis runs over, the one named last changes fastest.
Arguments:
- entering: bfloat16 [2, 512, 3584], P('section', 'expert'), may hold values from -6 to 6
- saved: bfloat16 [2, 16, 384, 384], P('section', 'expert'), may hold values from -6 to 6
- routes: int32 [2, 2, 512, 1], P(None, 'section', 'expert'), may hold values from 0 to 1; in each aligned block of 32 rows (0 to 31, 32 to 63, ..., all dimensions but the last counted through in order) at most 24 rows name the same one
- gates: float32 [2, 2, 512, 1], P(None, 'section', 'expert'), may hold values from 0.1 to 1
- w_in: bfloat16 [2, 16, 3584, 384], P('section', 'expert'), may hold values from -0.09375 to 0.09375
- w_out: bfloat16 [2, 16, 192, 3584], P('section', 'expert'), may hold values from -0.15625 to 0.15625
Outputs:
- results: bfloat16 [2, 2, 512, 3584], P(None, 'section', 'expert')
Inputs may be any that keep to these rules, and one draw needn't show every extreme that they name: `routes`: each row names one expert; in the rows of one device for one tick and layer no expert is named more than 24 times.
All inputs are finite; a program needn't handle non-finite values.
Results may differ from a plain program's by a relative error of at most 0.015.
Values may be sent and summed in bfloat16 or wider, within the bound.
A program may use at most 64 MiB of HBM per device.

v0:
```python
import jax
import jax.numpy as jnp
from jax import lax
from jax.sharding import PartitionSpec as P

SHARDS = 8


def shifted(shard, axis, by):
    devices = lax.axis_size(axis)
    pairs = [(i, i + by) for i in range(devices) if 0 <= i + by < devices]
    return lax.ppermute(shard, axis, pairs)


def silu_slope(gate_vals):
    sigmoid_vals = jax.nn.sigmoid(gate_vals)
    return sigmoid_vals * (1.0 + gate_vals * (1.0 - sigmoid_vals))


def routing_tables(routes, weights, experts, capacity):
    tok_count, top_count = routes.shape
    pair_count = tok_count * top_count
    flat_routes = routes.reshape(pair_count)
    expert_ids = jnp.arange(experts, dtype=jnp.int32)
    onehot = (flat_routes[:, None] == expert_ids[None, :]).astype(jnp.float32)
    pair_ids = jnp.arange(pair_count, dtype=jnp.int32)
    earlier = (pair_ids[None, :] < pair_ids[:, None]).astype(jnp.float32)
    before = jnp.dot(earlier, onehot, precision=lax.Precision.HIGHEST)
    slot_ids = jnp.sum(before * onehot, axis=1).astype(jnp.int32)
    targets = flat_routes * capacity + slot_ids
    slot_range = jnp.arange(experts * capacity, dtype=jnp.int32)
    places = (slot_range[:, None] == targets[None, :]).astype(jnp.float32)
    token_ids = jnp.arange(tok_count, dtype=jnp.int32)
    owners = ((pair_ids // top_count)[:, None] == token_ids[None, :]).astype(jnp.float32)
    sending = jnp.dot(places, owners, precision=lax.Precision.HIGHEST).astype(jnp.bfloat16)
    weighted = owners * weights.reshape(pair_count)[:, None]
    mixing = lax.dot_general(
        weighted, places, (((0,), (1,)), ((), ())), precision=lax.Precision.HIGHEST
    )
    return (sending, mixing)


def expert_forward(token_rows, w_in_dev, w_out_dev):
    pre_act = jnp.dot(token_rows, w_in_dev, preferred_element_type=jnp.float32)
    half_width = w_out_dev.shape[0]
    gate_vals = pre_act[:, :half_width]
    up_vals = pre_act[:, half_width:]
    hidden = (jax.nn.silu(gate_vals) * up_vals).astype(jnp.bfloat16)
    return jnp.dot(hidden, w_out_dev, preferred_element_type=jnp.float32).astype(jnp.bfloat16)


def expert_backward(grad_rows, saved_pre, w_in_dev, w_out_dev):
    half_width = w_out_dev.shape[0]
    gate_vals = saved_pre[:, :half_width].astype(jnp.float32)
    up_vals = saved_pre[:, half_width:].astype(jnp.float32)
    d_hidden = lax.dot_general(
        grad_rows, w_out_dev, (((1,), (1,)), ((), ())), preferred_element_type=jnp.float32
    )
    d_gate = d_hidden * up_vals * silu_slope(gate_vals)
    d_up = d_hidden * jax.nn.silu(gate_vals)
    d_pre = jnp.concatenate([d_gate, d_up], axis=1).astype(jnp.bfloat16)
    return lax.dot_general(
        d_pre, w_in_dev, (((1,), (1,)), ((), ())), preferred_element_type=jnp.float32
    ).astype(jnp.bfloat16)


def shards(entering, saved, routes, gates, w_in, w_out):
    peer_count = lax.axis_size("expert")
    experts = peer_count // SHARDS
    tok_count = entering.shape[1]
    row_width = entering.shape[2]
    top_count = routes.shape[3]
    capacity = min(
        tok_count, max(2, (3 * tok_count * top_count + 2 * experts - 1) // (2 * experts))
    )
    w_in_dev = w_in[0, 0]
    w_out_dev = w_out[0, 0]
    saved_dev = saved[0, 0]
    section_idx = lax.axis_index("section")
    forward_first = section_idx % 2 == 0
    current = entering[0]
    collected = []

    def run_forward(arrived_rows):
        return expert_forward(arrived_rows, w_in_dev, w_out_dev)

    def run_backward(arrived_rows):
        return expert_backward(arrived_rows, saved_dev, w_in_dev, w_out_dev)

    for tick_idx in range(2):
        doing_forward = forward_first if tick_idx == 0 else jnp.logical_not(forward_first)
        sending, mixing = routing_tables(routes[tick_idx, 0], gates[tick_idx, 0], experts, capacity)
        token_rows = jnp.dot(sending, current, preferred_element_type=jnp.float32).astype(
            jnp.bfloat16
        )
        shaped = token_rows.reshape(experts, 1, capacity, row_width)
        copies = jnp.broadcast_to(shaped, (experts, SHARDS, capacity, row_width)).reshape(
            peer_count, capacity, row_width
        )
        arrived = lax.all_to_all(copies, "expert", split_axis=0, concat_axis=0, tiled=True)
        expert_out = lax.cond(
            doing_forward,
            run_forward,
            run_backward,
            arrived.reshape(peer_count * capacity, row_width),
        )
        returned = lax.all_to_all(
            expert_out.reshape(peer_count, capacity, row_width),
            "expert",
            split_axis=0,
            concat_axis=0,
            tiled=True,
        )
        summed = jnp.sum(
            returned.reshape(experts, SHARDS, capacity, row_width).astype(jnp.float32), axis=1
        )
        mixed_sum = jnp.dot(
            mixing, summed.reshape(experts * capacity, row_width), precision=lax.Precision.HIGHEST
        )
        layer_result = (current.astype(jnp.float32) + mixed_sum).astype(jnp.bfloat16)
        collected.append(layer_result)
        if tick_idx == 0:
            from_below = shifted(layer_result, "section", 1)
            from_above = shifted(layer_result, "section", -1)
            current = jnp.where(forward_first, from_above, from_below)
    return jnp.stack(collected)[:, None]


def solution(mesh):
    return jax.shard_map(
        shards,
        mesh=mesh,
        in_specs=(
            P("section", "expert", None),
            P("section", "expert", None, None),
            P(None, "section", "expert", None),
            P(None, "section", "expert", None),
            P("section", "expert", None, None),
            P("section", "expert", None, None),
        ),
        out_specs=P(None, "section", "expert", None),
        check_vma=False,
    )
```

profile of v0, /device:TPU:15, one launch (start us, length us, event | category | flops | bytes accessed | tf_op | source)
XLA Modules:
  0.0 302.6 jit_solution(15326595954339328542)
XLA Ops:
  1.0 0.7 convert_add_fusion.1
  1.8 1.2 convolution_convert_fusion.1
  2.9 1.8 broadcast_in_dim.11
  4.7 6.7 %all-to-all-start = ((bf16[16,24,3584]{2,1,0:T(8,128)(2,1)}), bf16[16,24,3584]{2,1,0:T(8,128)(2,1)}, u32[]{:S(2)}, u32[]{:S(2)}) async-start(bf16[16,24,3584]{2,1,0:T(8,128)(2,1)} %bitcast.4), calls=%async_computation | async-start | bytes 5505024 | tf_op jit(solution)/shard_map/all_to_all | solution.py:100
  11.4 0.9 copy.7
  12.3 60.7 %all-to-all-done = bf16[16,24,3584]{2,1,0:T(8,128)(2,1)} async-done(((bf16[16,24,3584]{2,1,0:T(8,128)(2,1)}), bf16[16,24,3584]{2,1,0:T(8,128)(2,1)}, u32[]{:S(2)}, u32[]{:S(2)}) %all-to-all-start) | async-done | bytes 2752544 | tf_op jit(solution)/shard_map/all_to_all | solution.py:100
  73.0 6.3 %conditional.4 = (bf16[384,3584]{1,0:T(8,128)(2,1)}) conditional(s32[]{:T(128)} %convert_element_type.96, (bf16[384,3584]{1,0:T(8,128)(2,1)}, bf16[192,3584]{1,0:T(8,128)(2,1)S(1)}, bf16[384,384]{0,1:T(8,128)(2,1)}, bf16[3584,384]{1,0:T(8,128)(2,1)}) %tuple.40, (bf16[384,3584]{1,0:T(8,128)(2,1)}, bf16[3584,384]{1,0:T(8,128)(2,1)}, ...), branch_computations={%region_1.2_spmd, %region_2.3_spmd} | conditional | flops 1587142656 | bytes 21528612
  73.0 3.1 %fusion.6 = (bf16[384,192]{0,1:T(8,128)(2,1)S(1)}, bf16[384,192]{0,1:T(8,128)(2,1)S(1)}) fusion(bf16[384,384]{0,1:T(8,128)(2,1)} %get-tuple-element.45, bf16[384,3584]{1,0:T(8,128)(2,1)} %get-tuple-element.43, bf16[192,3584]{1,0:T(8,128)(2,1)S(1)} %get-tuple-element.44), kind=kOutput, calls=%fused_computation.9 | convolution fusion | flops 529588224 | bytes 4718592 | tf_op jit(solution)/shard_map/cond/branch_0_fun/dot_general | solution.py:56
  76.1 3.2 %fusion.9 = bf16[384,3584]{1,0:T(8,128)(2,1)} fusion(bf16[3584,384]{1,0:T(8,128)(2,1)S(1)} %copy-done.5, bf16[384,192]{0,1:T(8,128)(2,1)S(1)} %get-tuple-element.58, bf16[384,192]{0,1:T(8,128)(2,1)S(1)} %get-tuple-element.57), kind=kOutput, calls=%fused_computation.12 | convolution fusion | flops 1057554432 | bytes 5799936 | tf_op jit(solution)/shard_map/cond/branch_0_fun/dot_general | solution.py:62
  79.3 5.0 %all-to-all-start.1 = ((bf16[16,24,3584]{2,1,0:T(8,128)(2,1)}), bf16[16,24,3584]{2,1,0:T(8,128)(2,1)S(1)}, u32[]{:S(2)}, u32[]{:S(2)}) async-start(bf16[16,24,3584]{2,1,0:T(8,128)(2,1)} %bitcast.9), calls=%async_computation.1 | async-start | bytes 5505024 | tf_op jit(solution)/shard_map/all_to_all | solution.py:107
  84.6 61.2 %all-to-all-done.1 = bf16[16,24,3584]{2,1,0:T(8,128)(2,1)S(1)} async-done(((bf16[16,24,3584]{2,1,0:T(8,128)(2,1)}), bf16[16,24,3584]{2,1,0:T(8,128)(2,1)S(1)}, u32[]{:S(2)}, u32[]{:S(2)}) %all-to-all-start.1) | async-done | bytes 2752544 | tf_op jit(solution)/shard_map/all_to_all | solution.py:107
  146.8 2.6 collective-permute-start
  149.4 1.3 collective-permute-start.1
  150.8 3.3 %collective-permute-done = bf16[32,3584]{1,0:T(8,128)(2,1)S(1)} collective-permute-done((bf16[32,3584]{1,0:T(8,128)(2,1)S(1)}, bf16[32,3584]{1,0:T(8,128)(2,1)S(1)}, u32[]{:S(2)}, u32[]{:S(2)}) %collective-permute-start) | collective-permute-done | bytes 229408 | tf_op jit(solution)/shard_map/ppermute | solution.py:12
  154.1 3.8 %collective-permute-done.1 = bf16[32,3584]{1,0:T(8,128)(2,1)S(1)} collective-permute-done((bf16[32,3584]{1,0:T(8,128)(2,1)S(1)}, bf16[32,3584]{1,0:T(8,128)(2,1)S(1)}, u32[]{:S(2)}, u32[]{:S(2)}) %collective-permute-start.1) | collective-permute-done | bytes 229408 | tf_op jit(solution)/shard_map/ppermute | solution.py:12
  158.2 1.8 broadcast_in_dim.13
  160.0 6.2 %all-to-all-start.2 = ((bf16[16,24,3584]{2,1,0:T(8,128)(2,1)}), bf16[16,24,3584]{2,1,0:T(8,128)(2,1)}, u32[]{:S(2)}, u32[]{:S(2)}) async-start(bf16[16,24,3584]{2,1,0:T(8,128)(2,1)} %bitcast.16), calls=%async_computation.2 | async-start | bytes 5505024 | tf_op jit(solution)/shard_map/all_to_all | solution.py:100
  166.1 61.6 %all-to-all-done.2 = bf16[16,24,3584]{2,1,0:T(8,128)(2,1)} async-done(((bf16[16,24,3584]{2,1,0:T(8,128)(2,1)}), bf16[16,24,3584]{2,1,0:T(8,128)(2,1)}, u32[]{:S(2)}, u32[]{:S(2)}) %all-to-all-start.2) | async-done | bytes 2752544 | tf_op jit(solution)/shard_map/all_to_all | solution.py:100
  227.7 6.8 %conditional.5 = (bf16[384,3584]{1,0:T(8,128)(2,1)}) conditional(s32[]{:T(128)} %convert_element_type.105, (bf16[384,3584]{1,0:T(8,128)(2,1)}, bf16[192,3584]{1,0:T(8,128)(2,1)S(1)}, bf16[384,384]{0,1:T(8,128)(2,1)}, bf16[3584,384]{1,0:T(8,128)(2,1)}) %tuple.42, (bf16[384,3584]{1,0:T(8,128)(2,1)}, bf16[3584,384]{1,0:T(8,128)(2,1)}, ...), branch_computations={%region_5.6_spmd, %region_6.7_spmd} | conditional | flops 1587142656 | bytes 21528612
  227.7 4.2 %fusion.64 = f32[384,384]{0,1:T(8,128)S(1)} fusion(bf16[384,3584]{1,0:T(8,128)(2,1)} %get-tuple-element.54, bf16[3584,384]{1,0:T(8,128)(2,1)} %get-tuple-element.55), kind=kOutput, calls=%fused_computation.92 | convolution fusion | flops 1056964608 | bytes 6094848 | tf_op jit(solution)/shard_map/cond/branch_1_fun/dot_general | solution.py:44
  231.9 2.5 fusion.34
  234.5 4.9 %all-to-all-start.3 = ((bf16[16,24,3584]{2,1,0:T(8,128)(2,1)}), bf16[16,24,3584]{2,1,0:T(8,128)(2,1)S(1)}, u32[]{:S(2)}, u32[]{:S(2)}) async-start(bf16[16,24,3584]{2,1,0:T(8,128)(2,1)} %bitcast.18), calls=%async_computation.3 | async-start | bytes 5505024 | tf_op jit(solution)/shard_map/all_to_all | solution.py:107
  239.6 61.2 %all-to-all-done.3 = bf16[16,24,3584]{2,1,0:T(8,128)(2,1)S(1)} async-done(((bf16[16,24,3584]{2,1,0:T(8,128)(2,1)}), bf16[16,24,3584]{2,1,0:T(8,128)(2,1)S(1)}, u32[]{:S(2)}, u32[]{:S(2)}) %all-to-all-start.3) | async-done | bytes 2752544 | tf_op jit(solution)/shard_map/all_to_all | solution.py:107
  301.8 0.8 maximum_bitcast_fusion
  (25 shorter events, 3.8 us)
Async XLA Ops:
  4.7 6.7 %copy-start.3 = (bf16[1,1,384,384]{3,2,1,0:T(8,128)(2,1)S(1)}, bf16[1,1,384,384]{3,2,1,0:T(8,128)(2,1)}, u32[]{:S(2)}) copy-start(bf16[1,1,384,384]{3,2,1,0:T(8,128)(2,1)} %param.11) | copy-start | bytes 884740
  4.7 68.3 %copy-start = (bf16[1,1,192,3584]{3,2,1,0:T(8,128)(2,1)S(1)}, bf16[1,1,192,3584]{3,2,1,0:T(8,128)(2,1)}, u32[]{:S(2)}) copy-start(bf16[1,1,192,3584]{3,2,1,0:T(8,128)(2,1)} %param.15) | copy-start | bytes 4128772
  4.7 68.3 %all-to-all-start = ((bf16[16,24,3584]{2,1,0:T(8,128)(2,1)}), bf16[16,24,3584]{2,1,0:T(8,128)(2,1)}, u32[]{:S(2)}, u32[]{:S(2)}) async-start(bf16[16,24,3584]{2,1,0:T(8,128)(2,1)} %bitcast.4), calls=%async_computation | async-start | bytes 5505024 | tf_op jit(solution)/shard_map/all_to_all | solution.py:100
  73.0 3.1 %copy-start.5 = (bf16[3584,384]{1,0:T(8,128)(2,1)S(1)}, bf16[3584,384]{1,0:T(8,128)(2,1)}, u32[]{:S(2)}) copy-start(bf16[3584,384]{1,0:T(8,128)(2,1)} %get-tuple-element.46) | copy-start | bytes 8257540 | tf_op jit(solution)/shard_map/conditional
  79.3 5.0 %copy-start.4 = (f32[2,1,32,1]{2,3,1,0:T(1,128)S(1)}, f32[2,1,32,1]{2,3,1,0:T(1,128)}, u32[]{:S(2)}) copy-start(f32[2,1,32,1]{2,3,1,0:T(1,128)} %param.13) | copy-start | bytes 772
  79.3 66.5 %all-to-all-start.1 = ((bf16[16,24,3584]{2,1,0:T(8,128)(2,1)}), bf16[16,24,3584]{2,1,0:T(8,128)(2,1)S(1)}, u32[]{:S(2)}, u32[]{:S(2)}) async-start(bf16[16,24,3584]{2,1,0:T(8,128)(2,1)} %bitcast.9), calls=%async_computation.1 | async-start | bytes 5505024 | tf_op jit(solution)/shard_map/all_to_all | solution.py:107
  84.4 61.8 %copy-start.2 = (bf16[1,32,3584]{2,1,0:T(8,128)(2,1)S(1)}, bf16[1,32,3584]{2,1,0:T(8,128)(2,1)}, u32[]{:S(2)}) copy-start(bf16[1,32,3584]{2,1,0:T(8,128)(2,1)} %param.10) | copy-start | bytes 688132
  146.8 7.4 %collective-permute-start = (bf16[32,3584]{1,0:T(8,128)(2,1)S(1)}, bf16[32,3584]{1,0:T(8,128)(2,1)S(1)}, u32[]{:S(2)}, u32[]{:S(2)}) collective-permute-start(bf16[32,3584]{1,0:T(8,128)(2,1)S(1)} %fusion.38), channel_id=1, source_target_pairs={{16,0},{17,1},{18,2},{19,3},{20,4},{21,5},{22,6},{23,7},{24,8},{25... | collective-permute-start | bytes 688136 | tf_op jit(solution)/shard_map/ppermute | solution.py:12
  149.4 8.6 %collective-permute-start.1 = (bf16[32,3584]{1,0:T(8,128)(2,1)S(1)}, bf16[32,3584]{1,0:T(8,128)(2,1)S(1)}, u32[]{:S(2)}, u32[]{:S(2)}) collective-permute-start(bf16[32,3584]{1,0:T(8,128)(2,1)S(1)} %fusion.38), channel_id=1, source_target_pairs={{0,16},{1,17},{2,18},{3,19},{4,20},{5,21},{6,22},{7,23},{8,24},{9,... | collective-permute-start | bytes 688136 | tf_op jit(solution)/shard_map/ppermute | solution.py:12
  160.0 67.7 %copy-start.1 = (bf16[1,1,192,3584]{3,2,1,0:T(8,128)(2,1)S(1)}, bf16[1,1,192,3584]{3,2,1,0:T(8,128)(2,1)}, u32[]{:S(2)}) copy-start(bf16[1,1,192,3584]{3,2,1,0:T(8,128)(2,1)} %param.15) | copy-start | bytes 4128772
  160.0 67.7 %all-to-all-start.2 = ((bf16[16,24,3584]{2,1,0:T(8,128)(2,1)}), bf16[16,24,3584]{2,1,0:T(8,128)(2,1)}, u32[]{:S(2)}, u32[]{:S(2)}) async-start(bf16[16,24,3584]{2,1,0:T(8,128)(2,1)} %bitcast.16), calls=%async_computation.2 | async-start | bytes 5505024 | tf_op jit(solution)/shard_map/all_to_all | solution.py:100
  234.5 66.4 %all-to-all-start.3 = ((bf16[16,24,3584]{2,1,0:T(8,128)(2,1)}), bf16[16,24,3584]{2,1,0:T(8,128)(2,1)S(1)}, u32[]{:S(2)}, u32[]{:S(2)}) async-start(bf16[16,24,3584]{2,1,0:T(8,128)(2,1)} %bitcast.18), calls=%async_computation.3 | async-start | bytes 5505024 | tf_op jit(solution)/shard_map/all_to_all | solution.py:107
where the time goes:
time: 303 us
  waiting for transfers between devices  252 us (83%)
  starting transfers between devices  26.7 us (9%)
  matrix products  16.6 us (5%)
  local copies, waits for them, and re-layouts  5.16 us (2%)
    all_to_all x2, waiting for transfers between devices, shards(): lax.all_to_all(expert_out.reshape(peer_count, capacity, row_width), 'expe...  122 us
    all_to_all x2, waiting for transfers between devices, shards(): lax.all_to_all(copies, 'expert', split_axis=0, concat_axis=0, tiled=True)  122 us
    all_to_all x2, starting transfers between devices, shards(): lax.all_to_all(copies, 'expert', split_axis=0, concat_axis=0, tiled=True)  12.9 us
    all_to_all x2, starting transfers between devices, shards(): lax.all_to_all(expert_out.reshape(peer_count, capacity, row_width), 'expe...  9.95 us
    ppermute x2, waiting for transfers between devices, shifted(): return lax.ppermute(shard, axis, pairs)  7.15 us
  transfers between devices with their start and end apart: 6, of which 6 were waited for; matrix products, arithmetic and copies ran while one was open for 1% of the time, Pallas kernels for 0%

commit v1 on v0

v1 whole, which is shorter than its diff:
```python
import functools

import jax
import jax.numpy as jnp
from jax import lax
from jax.experimental import pallas as pl
from jax.experimental.pallas import tpu as pltpu
from jax.sharding import PartitionSpec as P

SHARDS = 8
CHIPS = 4
CHUNKS = 4
MESH = pl.DeviceIdType.MESH
F32 = jnp.float32
BF16 = jnp.bfloat16


def silu_slope(gate_vals):
    sigmoid_vals = jax.nn.sigmoid(gate_vals)
    return sigmoid_vals * (1.0 + gate_vals * (1.0 - sigmoid_vals))


def nn(a, b):
    return jnp.dot(a, b, preferred_element_type=F32)


def nt(a, b):
    return lax.dot_general(a, b, (((1,), (1,)), ((), ())), preferred_element_type=F32)


def tn(a, b):
    return lax.dot_general(a, b, (((0,), (0,)), ((), ())), preferred_element_type=F32)


def iota(shape, dim):
    return lax.broadcasted_iota(jnp.int32, shape, dim)


def wavefront(stages, chunks):
    for step in range(chunks + len(stages) - 1):
        for number in reversed(range(len(stages))):
            if 0 <= step - number < chunks:
                stages[number](step - number)


def kernel(
    experts, cap, cp, entering, routes, gates, saved_hbm, w_in_hbm, w_out_hbm, out,
    w_in, w_out, saved, silu_g, slope_u, acc, act, place, merge,
    gbuf, rbuf, agbuf, pbuf, sibbuf, qbuf, rsbuf, ubuf, vbuf, xbuf,
    load_sem, cross_s, cross_r, ag_s, ag_r, fw_s, fw_r, sib_s, sib_r,
    rs_s, rs_r, ret_s, ret_r, x_s, x_r,
):
    sec = lax.axis_index("section")
    me = lax.axis_index("expert")
    e, j = lax.div(me, SHARDS), lax.rem(me, SHARDS)
    q, c = lax.div(j, 2), lax.rem(j, 2)
    parity = lax.rem(sec, 2)
    tok, width = entering.shape
    dk = width // CHUNKS
    rows = experts * cap
    half = CHIPS * rows
    hdev = w_out.shape[0]

    def at_expert(o):
        return (sec, lax.rem(e + o, experts) * SHARDS + j)

    def at_chip(o):
        return (sec, e * SHARDS + lax.rem(q + o, CHIPS) * 2 + c)

    sibling = (sec, me + 1 - 2 * c)
    partner = (sec + 1 - 2 * parity, me)

    loads = [
        pltpu.make_async_copy(src, dst, load_sem.at[i])
        for i, (src, dst) in enumerate(
            ((saved_hbm, saved), (w_in_hbm, w_in), (w_out_hbm, w_out))
        )
    ]
    for load in loads:
        load.start()

    barrier = pltpu.get_barrier_semaphore()
    greeted = (
        [at_expert(o) for o in range(1, experts)]
        + [at_chip(o) for o in range(1, CHIPS)]
        + [sibling, partner]
    )
    for device in greeted:
        pl.semaphore_signal(barrier, inc=1, device_id=device, device_id_type=MESH)

    earlier = (iota((tok, tok), 1) < iota((tok, tok), 0)).astype(BF16)
    for tick in range(2):
        onehot = (routes[tick] == iota((tok, 128), 1)).astype(F32)
        before = nn(earlier, onehot.astype(BF16))
        slot = jnp.sum(before * onehot, axis=1, keepdims=True).astype(jnp.int32)
        target = routes[tick] * cp + slot
        place[tick] = (target == iota((tok, experts * cp), 1)).astype(F32).astype(BF16)
    r = iota((rows, experts * cp), 0)
    merge[...] = (
        (r // cap * cp + r % cap == iota((rows, experts * cp), 1)).astype(F32).astype(BF16)
    )

    pl.semaphore_wait(barrier, len(greeted))

    def copy(src, dst, send, recv, device):
        return pltpu.make_async_remote_copy(
            src_ref=src, dst_ref=dst, send_sem=send, recv_sem=recv,
            device_id=device, device_id_type=MESH,
        )

    sent = []

    def send(src, dst, send_sem, recv_sem, device):
        one = copy(src, dst, send_sem, recv_sem, device)
        one.start()
        sent.append(one)

    def arrive(dst, send_sem, recv_sem, device):
        copy(dst, dst, send_sem, recv_sem, device).wait_recv()

    def ds(index, size):
        return pl.ds(pl.multiple_of(index * size, size), size)

    def cols(k):
        return slice(k * dk, (k + 1) * dk)

    def tokens(t, k):
        return entering[:, cols(k)] if t == 0 else xbuf[k]

    def prepare_saved():
        for load in loads:
            load.wait()
        total = SHARDS * rows
        r = iota((total, total), 0)
        block, inner = r // rows, r % rows
        source_j = block % CHIPS * 2 + block // CHIPS
        column = (inner // cap * SHARDS + source_j) * cap + inner % cap
        perm = (column == iota((total, total), 1)).astype(F32).astype(BF16)
        ordered = nn(perm, saved[...])
        gate_vals, up_vals = ordered[:, :hdev], ordered[:, hdev:]
        silu_g[...] = jax.nn.silu(gate_vals)
        slope_u[...] = up_vals * silu_slope(gate_vals)

    def dispatch(t, forward):
        def spread(k):
            if t == 1:
                arrive(xbuf.at[k], x_s.at[k], x_r.at[k], partner)
            gbuf[t, k] = tn(place[t], tokens(t, k)).astype(BF16)
            for o in range(1, experts):
                send(
                    gbuf.at[t, k, ds(lax.rem(e + o, experts), cp)],
                    rbuf.at[t, k, ds(e, cp)],
                    cross_s.at[t, k, o], cross_r.at[t, k, o], at_expert(o),
                )
            rbuf[t, k, ds(e, cp)] = gbuf[t, k, ds(e, cp)]

        def gather(k):
            for o in range(1, experts):
                arrive(
                    rbuf.at[t, k, ds(lax.rem(e + experts - o, experts), cp)],
                    cross_s.at[t, k, o], cross_r.at[t, k, o], at_expert(o),
                )
            mine = ds(c * CHIPS + q, rows)
            agbuf[t, k, mine] = nn(merge[...], rbuf[t, k]).astype(BF16)
            for o in range(1, CHIPS):
                send(
                    agbuf.at[t, k, mine], agbuf.at[t, k, mine],
                    ag_s.at[t, k, o], ag_r.at[t, k, o], at_chip(o),
                )

        def forward_on(k):
            for o in range(1, CHIPS):
                arrive(
                    agbuf.at[t, k, ds(c * CHIPS + lax.rem(q + CHIPS - o, CHIPS), rows)],
                    ag_s.at[t, k, o], ag_r.at[t, k, o], at_chip(o),
                )
            send(
                agbuf.at[t, k, ds(c, half)], agbuf.at[t, k, ds(c, half)],
                fw_s.at[t, k], fw_r.at[t, k], sibling,
            )

        def multiply(k):
            if t == 0 and k == 0:
                prepare_saved()
            arrive(agbuf.at[t, k, ds(1 - c, half)], fw_s.at[t, k], fw_r.at[t, k], sibling)

            @pl.when(forward)
            def _():
                part = nn(agbuf[t, k], w_in[cols(k), :])
                acc[...] = part if k == 0 else acc[...] + part

            @pl.when(jnp.logical_not(forward))
            def _():
                part = nt(agbuf[t, k], w_out[:, cols(k)])
                acc[:, :hdev] = part if k == 0 else acc[:, :hdev] + part

            if k == CHUNKS - 1:
                activate(forward)

        return [spread, gather, forward_on, multiply]

    def activate(forward):
        @pl.when(forward)
        def _():
            hidden = jax.nn.silu(acc[:, :hdev]) * acc[:, hdev:]
            act[:, :hdev] = hidden.astype(BF16)

        @pl.when(jnp.logical_not(forward))
        def _():
            d_hidden = acc[:, :hdev]
            act[:, :hdev] = (d_hidden * slope_u[...]).astype(BF16)
            act[:, hdev:] = (d_hidden * silu_g[...]).astype(BF16)

    def give_back(t, forward):
        def part(k):
            @pl.when(forward)
            def _():
                pbuf[t, k] = nn(act[:, :hdev], w_out[:, cols(k)]).astype(BF16)

            @pl.when(jnp.logical_not(forward))
            def _():
                pbuf[t, k] = nt(act[...], w_in[cols(k), :]).astype(BF16)

            send(
                pbuf.at[t, k, ds(1 - c, half)], sibbuf.at[t, k],
                sib_s.at[t, k], sib_r.at[t, k], sibling,
            )

        def scatter(k):
            arrive(sibbuf.at[t, k], sib_s.at[t, k], sib_r.at[t, k], sibling)
            both = pbuf[t, k, ds(c, half)].astype(F32) + sibbuf[t, k].astype(F32)
            qbuf[t, k] = both.astype(BF16)
            for o in range(1, CHIPS):
                send(
                    qbuf.at[t, k, ds(lax.rem(q + o, CHIPS), rows)], rsbuf.at[t, k, o],
                    rs_s.at[t, k, o], rs_r.at[t, k, o], at_chip(o),
                )

        def return_on(k):
            total = qbuf[t, k, ds(q, rows)].astype(F32)
            for o in range(1, CHIPS):
                arrive(rsbuf.at[t, k, o], rs_s.at[t, k, o], rs_r.at[t, k, o], at_chip(o))
                total = total + rsbuf[t, k, o].astype(F32)
            ubuf[t, k] = tn(merge[...], total.astype(BF16)).astype(BF16)
            for o in range(1, experts):
                send(
                    ubuf.at[t, k, ds(lax.rem(e + o, experts), cp)],
                    vbuf.at[t, k, ds(e, cp)],
                    ret_s.at[t, k, o], ret_r.at[t, k, o], at_expert(o),
                )
            vbuf[t, k, ds(e, cp)] = ubuf[t, k, ds(e, cp)]

        def combine(k):
            for o in range(1, experts):
                arrive(
                    vbuf.at[t, k, ds(lax.rem(e + experts - o, experts), cp)],
                    ret_s.at[t, k, o], ret_r.at[t, k, o], at_expert(o),
                )
            picked = nn(place[t], vbuf[t, k])
            result = (tokens(t, k).astype(F32) + gates[t] * picked).astype(BF16)
            out[t, :, cols(k)] = result
            if t == 0:
                stage_x[k] = result
                send(stage_x.at[k], xbuf.at[k], x_s.at[k], x_r.at[k], partner)

        return [part, scatter, return_on, combine]

    stage_x, xbuf = xbuf.at[0], xbuf.at[1]
    first, second = parity == 0, parity == 1
    wavefront(dispatch(0, first), CHUNKS)
    wavefront(give_back(0, first) + dispatch(1, second), CHUNKS)
    wavefront(give_back(1, second), CHUNKS)
    for one in sent:
        one.wait_send()


def shards(entering, saved, routes, gates, w_in, w_out):
    experts = lax.axis_size("expert") // SHARDS
    tok, width = entering.shape[1:]
    top = routes.shape[3]
    assert top == 1
    cap = min(tok, max(2, (3 * tok * top + 2 * experts - 1) // (2 * experts)))
    cp = -(-cap // 16) * 16
    rows = experts * cap
    total = SHARDS * rows
    half = CHIPS * rows
    hdev = w_out.shape[2]
    dk = width // CHUNKS
    steps = (2, CHUNKS)
    dma = pltpu.SemaphoreType.DMA
    vmem = pl.BlockSpec(memory_space=pltpu.VMEM)
    hbm = pl.BlockSpec(memory_space=pl.ANY)
    out = pl.pallas_call(
        functools.partial(kernel, experts, cap, cp),
        out_shape=jax.ShapeDtypeStruct((2, tok, width), BF16),
        in_specs=[vmem] * 3 + [hbm] * 3,
        out_specs=vmem,
        scratch_shapes=[
            pltpu.VMEM(w_in.shape[2:], BF16),
            pltpu.VMEM(w_out.shape[2:], BF16),
            pltpu.VMEM((total, 2 * hdev), BF16),
            pltpu.VMEM((total, hdev), F32),
            pltpu.VMEM((total, hdev), F32),
            pltpu.VMEM((total, 2 * hdev), F32),
            pltpu.VMEM((total, 2 * hdev), BF16),
            pltpu.VMEM((2, tok, experts * cp), BF16),
            pltpu.VMEM((rows, experts * cp), BF16),
            pltpu.VMEM(steps + (experts * cp, dk), BF16),
            pltpu.VMEM(steps + (experts * cp, dk), BF16),
            pltpu.VMEM(steps + (total, dk), BF16),
            pltpu.VMEM(steps + (total, dk), BF16),
            pltpu.VMEM(steps + (half, dk), BF16),
            pltpu.VMEM(steps + (half, dk), BF16),
            pltpu.VMEM(steps + (CHIPS, rows, dk), BF16),
            pltpu.VMEM(steps + (experts * cp, dk), BF16),
            pltpu.VMEM(steps + (experts * cp, dk), BF16),
            pltpu.VMEM(steps + (tok, dk), BF16),
            dma((3,)),
            dma(steps + (experts,)), dma(steps + (experts,)),
            dma(steps + (CHIPS,)), dma(steps + (CHIPS,)),
            dma(steps), dma(steps),
            dma(steps), dma(steps),
            dma(steps + (CHIPS,)), dma(steps + (CHIPS,)),
            dma(steps + (experts,)), dma(steps + (experts,)),
            dma((CHUNKS,)), dma((CHUNKS,)),
        ],
        compiler_params=pltpu.CompilerParams(
            collective_id=0, has_side_effects=True, vmem_limit_bytes=56 * 1024 * 1024
        ),
    )(
        entering[0], routes[:, 0], gates[:, 0], saved[0, 0], w_in[0, 0], w_out[0, 0]
    )
    return out[:, None]


def solution(mesh):
    return jax.shard_map(
        shards,
        mesh=mesh,
        in_specs=(
            P("section", "expert", None),
            P("section", "expert", None, None),
            P(None, "section", "expert", None),
            P(None, "section", "expert", None),
            P("section", "expert", None, None),
            P("section", "expert", None, None),
        ),
        out_specs=P(None, "section", "expert", None),
        check_vma=False,
    )
```

time: 303 us -> 125 us (0.41)
  the two profiles are of different devices: /device:TPU:15 before, /device:TPU:0 now
where the time goes in v1:
time: 125 us
  Pallas kernels  120 us (96%)
  local copies, waits for them, and re-layouts  4.56 us (4%)
    pallas_call x1, Pallas kernels, shards(): pl.pallas_call(functools.partial(kernel, experts, cap, cp), out_shape=jax...  120 us

profile of v1, /device:TPU:0, one launch (start us, length us, event | category | flops | bytes accessed | tf_op | source)
XLA Modules:
  0.0 125.0 jit_solution(15076577840367583212)
XLA Ops:
  0.0 1.4 %copy.7.routes = s32[2,32,1]{2,1,0:T(8,128)} copy(s32[2,32,1]{1,0,2:T(2,128)} %bitcast.14) | data formatting | bytes 512 | tf_op jit(solution)/shard_map/squeeze | solution.py:331
  1.4 1.4 %copy.8.gates = f32[2,32,1]{2,1,0:T(8,128)} copy(f32[2,32,1]{1,0,2:T(2,128)} %bitcast.15) | data formatting | bytes 512 | tf_op jit(solution)/shard_map/squeeze | solution.py:331
  2.8 120.4 %shard_map.64 = bf16[2,32,3584]{2,1,0:T(8,128)(2,1)} custom-call(bf16[32,3584]{1,0:T(8,128)(2,1)} %bitcast.13, s32[2,32,1]{2,1,0:T(8,128)} %copy.7.routes, f32[2,32,1]{2,1,0:T(8,128)} %copy.8.gates, bf16[384,384]{1,0:T(8,128)(2,1)} %bitcast.12, bf16[3584,384]{1,0:T(8,128)(2,1)} %bitcast.9, bf16[192,3584]{1,0:T(8,128)(2,1)} %bitcast.11), custom_call_target="tpu_custom_call" | custom-call | tf_op jit(solution)/shard_map/pallas_call | solution.py:293
  123.2 1.8 %copy.11 = bf16[2,1,32,3584]{3,2,1,0:T(8,128)(2,1)} copy(bf16[2,1,32,3584]{3,2,1,0:T(8,128)(2,1)} %bitcast.10) | data formatting | bytes 917504

commit v2 on v1

--- a/solution.py
+++ b/solution.py
@@ -8,8 +8,7 @@
 from jax.sharding import PartitionSpec as P
 
 SHARDS = 8
-CHIPS = 4
-CHUNKS = 4
+CHUNKS = 7
 MESH = pl.DeviceIdType.MESH
 F32 = jnp.float32
 BF16 = jnp.bfloat16
@@ -37,37 +36,36 @@
 
 
 def wavefront(stages, chunks):
-    for step in range(chunks + len(stages) - 1):
-        for number in reversed(range(len(stages))):
-            if 0 <= step - number < chunks:
-                stages[number](step - number)
+    starts = [0] + [number + 1 for number in range(1, len(stages))]
+    for step in range(chunks + starts[-1]):
+        for stage, start in reversed(list(zip(stages, starts))):
+            if 0 <= step - start < chunks:
+                stage(step - start)
 
 
 def kernel(
     experts, cap, cp, entering, routes, gates, saved_hbm, w_in_hbm, w_out_hbm, out,
     w_in, w_out, saved, silu_g, slope_u, acc, act, place, merge,
-    gbuf, rbuf, agbuf, pbuf, sibbuf, qbuf, rsbuf, ubuf, vbuf, xbuf,
-    load_sem, cross_s, cross_r, ag_s, ag_r, fw_s, fw_r, sib_s, sib_r,
-    rs_s, rs_r, ret_s, ret_r, x_s, x_r,
+    gbuf, rbuf, agbuf, pbuf, sibbuf, qbuf, ybuf, hbuf, zbuf, ubuf, vbuf, xbuf,
+    load_sem, cross_s, cross_r, ret_s, ret_r, x_s, x_r, hop_s, hop_r,
 ):
     sec = lax.axis_index("section")
     me = lax.axis_index("expert")
     e, j = lax.div(me, SHARDS), lax.rem(me, SHARDS)
-    q, c = lax.div(j, 2), lax.rem(j, 2)
+    z, y, c = lax.div(j, 4), lax.rem(lax.div(j, 2), 2), lax.rem(j, 2)
     parity = lax.rem(sec, 2)
     tok, width = entering.shape
     dk = width // CHUNKS
     rows = experts * cap
-    half = CHIPS * rows
+    quarter, half = 2 * rows, 4 * rows
     hdev = w_out.shape[0]
 
     def at_expert(o):
         return (sec, lax.rem(e + o, experts) * SHARDS + j)
 
-    def at_chip(o):
-        return (sec, e * SHARDS + lax.rem(q + o, CHIPS) * 2 + c)
-
     sibling = (sec, me + 1 - 2 * c)
+    across_y = (sec, me + 2 - 4 * y)
+    across_z = (sec, me + 4 - 8 * z)
     partner = (sec + 1 - 2 * parity, me)
 
     loads = [
@@ -80,11 +78,8 @@
         load.start()
 
     barrier = pltpu.get_barrier_semaphore()
-    greeted = (
-        [at_expert(o) for o in range(1, experts)]
-        + [at_chip(o) for o in range(1, CHIPS)]
-        + [sibling, partner]
-    )
+    greeted = [at_expert(o) for o in range(1, experts)]
+    greeted += [sibling, across_y, across_z, partner]
     for device in greeted:
         pl.semaphore_signal(barrier, inc=1, device_id=device, device_id_type=MESH)
 
@@ -118,6 +113,12 @@
     def arrive(dst, send_sem, recv_sem, device):
         copy(dst, dst, send_sem, recv_sem, device).wait_recv()
 
+    def hop(src, dst, t, k, number, device):
+        send(src, dst, hop_s.at[t, k, number], hop_r.at[t, k, number], device)
+
+    def landed(dst, t, k, number, device):
+        arrive(dst, hop_s.at[t, k, number], hop_r.at[t, k, number], device)
+
     def ds(index, size):
         return pl.ds(pl.multiple_of(index * size, size), size)
 
@@ -128,12 +129,11 @@
         return entering[:, cols(k)] if t == 0 else xbuf[k]
 
     def prepare_saved():
-        for load in loads:
-            load.wait()
+        loads[0].wait()
         total = SHARDS * rows
         r = iota((total, total), 0)
         block, inner = r // rows, r % rows
-        source_j = block % CHIPS * 2 + block // CHIPS
+        source_j = block % 2 * 4 + block // 2 % 2 * 2 + block // 4
         column = (inner // cap * SHARDS + source_j) * cap + inner % cap
         perm = (column == iota((total, total), 1)).astype(F32).astype(BF16)
         ordered = nn(perm, saved[...])
@@ -153,6 +153,8 @@
                     cross_s.at[t, k, o], cross_r.at[t, k, o], at_expert(o),
                 )
             rbuf[t, k, ds(e, cp)] = gbuf[t, k, ds(e, cp)]
+            if t == 0 and k == 1:
+                prepare_saved()
 
         def gather(k):
             for o in range(1, experts):
@@ -160,29 +162,25 @@
                     rbuf.at[t, k, ds(lax.rem(e + experts - o, experts), cp)],
                     cross_s.at[t, k, o], cross_r.at[t, k, o], at_expert(o),
                 )
-            mine = ds(c * CHIPS + q, rows)
-            agbuf[t, k, mine] = nn(merge[...], rbuf[t, k]).astype(BF16)
-            for o in range(1, CHIPS):
-                send(
-                    agbuf.at[t, k, mine], agbuf.at[t, k, mine],
-                    ag_s.at[t, k, o], ag_r.at[t, k, o], at_chip(o),
-                )
-
-        def forward_on(k):
-            for o in range(1, CHIPS):
-                arrive(
-                    agbuf.at[t, k, ds(c * CHIPS + lax.rem(q + CHIPS - o, CHIPS), rows)],
-                    ag_s.at[t, k, o], ag_r.at[t, k, o], at_chip(o),
-                )
-            send(
-                agbuf.at[t, k, ds(c, half)], agbuf.at[t, k, ds(c, half)],
-                fw_s.at[t, k], fw_r.at[t, k], sibling,
-            )
+            own = ds(c * 4 + y * 2 + z, rows)
+            agbuf[t, k, own] = nn(merge[...], rbuf[t, k]).astype(BF16)
+            hop(agbuf.at[t, k, own], agbuf.at[t, k, own], t, k, 0, across_z)
+
+        def over_y(k):
+            landed(agbuf.at[t, k, ds(c * 4 + y * 2 + 1 - z, rows)], t, k, 0, across_z)
+            pair = agbuf.at[t, k, ds(c * 2 + y, quarter)]
+            hop(pair, pair, t, k, 1, across_y)
+
+        def over_core(k):
+            landed(agbuf.at[t, k, ds(c * 2 + 1 - y, quarter)], t, k, 1, across_y)
+            mine = agbuf.at[t, k, ds(c, half)]
+            hop(mine, mine, t, k, 2, sibling)
 
         def multiply(k):
             if t == 0 and k == 0:
-                prepare_saved()
-            arrive(agbuf.at[t, k, ds(1 - c, half)], fw_s.at[t, k], fw_r.at[t, k], sibling)
+                loads[1].wait()
+                loads[2].wait()
+            landed(agbuf.at[t, k, ds(1 - c, half)], t, k, 2, sibling)
 
             @pl.when(forward)
             def _():
@@ -197,7 +195,7 @@
             if k == CHUNKS - 1:
                 activate(forward)
 
-        return [spread, gather, forward_on, multiply]
+        return [spread, gather, over_y, over_core, multiply]
 
     def activate(forward):
         @pl.when(forward)
@@ -221,26 +219,23 @@
             def _():
                 pbuf[t, k] = nt(act[...], w_in[cols(k), :]).astype(BF16)
 
-            send(
-                pbuf.at[t, k, ds(1 - c, half)], sibbuf.at[t, k],
-                sib_s.at[t, k], sib_r.at[t, k], sibling,
-            )
-
-        def scatter(k):
-            arrive(sibbuf.at[t, k], sib_s.at[t, k], sib_r.at[t, k], sibling)
+            hop(pbuf.at[t, k, ds(1 - c, half)], sibbuf.at[t, k], t, k, 3, sibling)
+
+        def scatter_y(k):
+            landed(sibbuf.at[t, k], t, k, 3, sibling)
             both = pbuf[t, k, ds(c, half)].astype(F32) + sibbuf[t, k].astype(F32)
             qbuf[t, k] = both.astype(BF16)
-            for o in range(1, CHIPS):
-                send(
-                    qbuf.at[t, k, ds(lax.rem(q + o, CHIPS), rows)], rsbuf.at[t, k, o],
-                    rs_s.at[t, k, o], rs_r.at[t, k, o], at_chip(o),
-                )
+            hop(qbuf.at[t, k, ds(1 - y, quarter)], ybuf.at[t, k], t, k, 4, across_y)
+
+        def scatter_z(k):
+            landed(ybuf.at[t, k], t, k, 4, across_y)
+            both = qbuf[t, k, ds(y, quarter)].astype(F32) + ybuf[t, k].astype(F32)
+            hbuf[t, k] = both.astype(BF16)
+            hop(hbuf.at[t, k, ds(1 - z, rows)], zbuf.at[t, k], t, k, 5, across_z)
 
         def return_on(k):
-            total = qbuf[t, k, ds(q, rows)].astype(F32)
-            for o in range(1, CHIPS):
-                arrive(rsbuf.at[t, k, o], rs_s.at[t, k, o], rs_r.at[t, k, o], at_chip(o))
-                total = total + rsbuf[t, k, o].astype(F32)
+            landed(zbuf.at[t, k], t, k, 5, across_z)
+            total = hbuf[t, k, ds(z, rows)].astype(F32) + zbuf[t, k].astype(F32)
             ubuf[t, k] = tn(merge[...], total.astype(BF16)).astype(BF16)
             for o in range(1, experts):
                 send(
@@ -263,7 +258,7 @@
                 stage_x[k] = result
                 send(stage_x.at[k], xbuf.at[k], x_s.at[k], x_r.at[k], partner)
 
-        return [part, scatter, return_on, combine]
+        return [part, scatter_y, scatter_z, return_on, combine]
 
     stage_x, xbuf = xbuf.at[0], xbuf.at[1]
     first, second = parity == 0, parity == 1
@@ -283,7 +278,7 @@
     cp = -(-cap // 16) * 16
     rows = experts * cap
     total = SHARDS * rows
-    half = CHIPS * rows
+    quarter, half = 2 * rows, 4 * rows
     hdev = w_out.shape[2]
     dk = width // CHUNKS
     steps = (2, CHUNKS)
@@ -311,18 +306,17 @@
             pltpu.VMEM(steps + (total, dk), BF16),
             pltpu.VMEM(steps + (half, dk), BF16),
             pltpu.VMEM(steps + (half, dk), BF16),
-            pltpu.VMEM(steps + (CHIPS, rows, dk), BF16),
+            pltpu.VMEM(steps + (quarter, dk), BF16),
+            pltpu.VMEM(steps + (quarter, dk), BF16),
+            pltpu.VMEM(steps + (rows, dk), BF16),
             pltpu.VMEM(steps + (experts * cp, dk), BF16),
             pltpu.VMEM(steps + (experts * cp, dk), BF16),
             pltpu.VMEM(steps + (tok, dk), BF16),
             dma((3,)),
             dma(steps + (experts,)), dma(steps + (experts,)),
-            dma(steps + (CHIPS,)), dma(steps + (CHIPS,)),
-            dma(steps), dma(steps),
-            dma(steps), dma(steps),
-            dma(steps + (CHIPS,)), dma(steps + (CHIPS,)),
             dma(steps + (experts,)), dma(steps + (experts,)),
             dma((CHUNKS,)), dma((CHUNKS,)),
+            dma(steps + (6,)), dma(steps + (6,)),
         ],
         compiler_params=pltpu.CompilerParams(
             collective_id=0, has_side_effects=True, vmem_limit_bytes=56 * 1024 * 1024

time: 125 us -> 143 us (1.14)
  Pallas kernels: 120 us -> 138 us
    pallas_call x1, Pallas kernels: 120 us -> 138 us  [shards(): pl.pallas_call(functools.partial(kernel, experts, cap, cp), out_shape=jax...]
where the time goes in v2:
time: 143 us
  Pallas kernels  138 us (97%)
  local copies, waits for them, and re-layouts  4.56 us (3%)
    pallas_call x1, Pallas kernels, shards(): pl.pallas_call(functools.partial(kernel, experts, cap, cp), out_shape=jax...  138 us

profile of v2, /device:TPU:0, one launch (start us, length us, event | category | flops | bytes accessed | tf_op | source)
XLA Modules:
  0.0 142.7 jit_solution(6462238632481644072)
XLA Ops:
  0.0 1.4 copy.7.routes
  1.4 1.4 copy.8.gates
  2.8 138.1 %shard_map.64 = bf16[2,32,3584]{2,1,0:T(8,128)(2,1)} custom-call(bf16[32,3584]{1,0:T(8,128)(2,1)} %bitcast.13, s32[2,32,1]{2,1,0:T(8,128)} %copy.7.routes, f32[2,32,1]{2,1,0:T(8,128)} %copy.8.gates, bf16[384,384]{1,0:T(8,128)(2,1)} %bitcast.12, bf16[3584,384]{1,0:T(8,128)(2,1)} %bitcast.9, bf16[192,3584]{1,0:T(8,128)(2,1)} %bitcast.11), custom_call_target="tpu_custom_call" | custom-call | tf_op jit(solution)/shard_map/pallas_call | solution.py:288
  140.9 1.8 %copy.11 = bf16[2,1,32,3584]{3,2,1,0:T(8,128)(2,1)} copy(bf16[2,1,32,3584]{3,2,1,0:T(8,128)(2,1)} %bitcast.10) | data formatting | bytes 917504

commit v3 on v1

--- a/solution.py
+++ b/solution.py
@@ -9,7 +9,10 @@
 
 SHARDS = 8
 CHIPS = 4
-CHUNKS = 4
+CHUNKS = 7
+HOP_US = 1.5
+STEP_US = 0.3
+LINK_RATE = {"y": 5e4, "z": 5e4, "mid": 5e4, "x": 5e4, "core": 6e5}
 MESH = pl.DeviceIdType.MESH
 F32 = jnp.float32
 BF16 = jnp.bfloat16
@@ -36,16 +39,29 @@
     return lax.broadcasted_iota(jnp.int32, shape, dim)
 
 
-def wavefront(stages, chunks):
-    for step in range(chunks + len(stages) - 1):
-        for number in reversed(range(len(stages))):
-            if 0 <= step - number < chunks:
-                stages[number](step - number)
+def listed(stages, chunks, row_bytes):
+    now, free, done = 0.0, {}, [0] * len(stages)
+    arrival = {(0, k): 0.0 for k in range(chunks)}
+    for _ in range(len(stages) * chunks):
+        open_now = [
+            (number, k) for number, k in enumerate(done) if k < chunks and (number, k) in arrival
+        ]
+        ready = [item for item in open_now if arrival[item] <= now]
+        number, k = max(ready) if ready else min(open_now, key=lambda item: arrival[item])
+        stage, work, sends = stages[number]
+        stage(k)
+        done[number] += 1
+        now = max(now, arrival[number, k]) + STEP_US + work / chunks
+        arrived = now
+        for link, rows in sends:
+            free[link] = max(now, free.get(link, 0.0)) + rows * row_bytes / LINK_RATE[link]
+            arrived = max(arrived, free[link] + HOP_US)
+        arrival[number + 1, k] = arrived
 
 
 def kernel(
     experts, cap, cp, entering, routes, gates, saved_hbm, w_in_hbm, w_out_hbm, out,
-    w_in, w_out, saved, silu_g, slope_u, acc, act, place, merge,
+    w_in, w_out, saved, silu_g, slope_u, acc, act, weight, place, merge,
     gbuf, rbuf, agbuf, pbuf, sibbuf, qbuf, rsbuf, ubuf, vbuf, xbuf,
     load_sem, cross_s, cross_r, ag_s, ag_r, fw_s, fw_r, sib_s, sib_r,
     rs_s, rs_r, ret_s, ret_r, x_s, x_r,
@@ -89,11 +105,18 @@
         pl.semaphore_signal(barrier, inc=1, device_id=device, device_id_type=MESH)
 
     earlier = (iota((tok, tok), 1) < iota((tok, tok), 0)).astype(BF16)
+    same = iota((tok, tok), 1) == iota((tok, tok), 0)
+
+    def column(row):
+        return jnp.sum(jnp.where(same, row.astype(F32), 0.0), axis=1, keepdims=True)
+
     for tick in range(2):
-        onehot = (routes[tick] == iota((tok, 128), 1)).astype(F32)
+        route = column(routes[tick]).astype(jnp.int32)
+        weight[tick] = column(gates[tick])
+        onehot = (route == iota((tok, 128), 1)).astype(F32)
         before = nn(earlier, onehot.astype(BF16))
         slot = jnp.sum(before * onehot, axis=1, keepdims=True).astype(jnp.int32)
-        target = routes[tick] * cp + slot
+        target = route * cp + slot
         place[tick] = (target == iota((tok, experts * cp), 1)).astype(F32).astype(BF16)
     r = iota((rows, experts * cp), 0)
     merge[...] = (
@@ -128,8 +151,7 @@
         return entering[:, cols(k)] if t == 0 else xbuf[k]
 
     def prepare_saved():
-        for load in loads:
-            load.wait()
+        loads[0].wait()
         total = SHARDS * rows
         r = iota((total, total), 0)
         block, inner = r // rows, r % rows
@@ -153,6 +175,8 @@
                     cross_s.at[t, k, o], cross_r.at[t, k, o], at_expert(o),
                 )
             rbuf[t, k, ds(e, cp)] = gbuf[t, k, ds(e, cp)]
+            if t == 0 and k == 2:
+                prepare_saved()
 
         def gather(k):
             for o in range(1, experts):
@@ -181,7 +205,8 @@
 
         def multiply(k):
             if t == 0 and k == 0:
-                prepare_saved()
+                loads[1].wait()
+                loads[2].wait()
             arrive(agbuf.at[t, k, ds(1 - c, half)], fw_s.at[t, k], fw_r.at[t, k], sibling)
 
             @pl.when(forward)
@@ -197,7 +222,12 @@
             if k == CHUNKS - 1:
                 activate(forward)
 
-        return [spread, gather, forward_on, multiply]
+        return [
+            (spread, 1.0, [("z", cp), ("mid", 2 * cp)]),
+            (gather, 1.0, [("y", 2 * rows), ("z", 2 * rows)]),
+            (forward_on, 0.0, [("core", half)]),
+            (multiply, 4.0, []),
+        ]
 
     def activate(forward):
         @pl.when(forward)
@@ -257,19 +287,24 @@
                     ret_s.at[t, k, o], ret_r.at[t, k, o], at_expert(o),
                 )
             picked = nn(place[t], vbuf[t, k])
-            result = (tokens(t, k).astype(F32) + gates[t] * picked).astype(BF16)
+            result = (tokens(t, k).astype(F32) + weight[t] * picked).astype(BF16)
             out[t, :, cols(k)] = result
             if t == 0:
                 stage_x[k] = result
                 send(stage_x.at[k], xbuf.at[k], x_s.at[k], x_r.at[k], partner)
 
-        return [part, scatter, return_on, combine]
+        return [
+            (part, 4.0, [("core", half)]),
+            (scatter, 1.5, [("y", 2 * rows), ("z", 2 * rows)]),
+            (return_on, 1.0, [("z", cp), ("mid", 2 * cp)]),
+            (combine, 0.7, [("x", tok)]),
+        ]
 
     stage_x, xbuf = xbuf.at[0], xbuf.at[1]
     first, second = parity == 0, parity == 1
-    wavefront(dispatch(0, first), CHUNKS)
-    wavefront(give_back(0, first) + dispatch(1, second), CHUNKS)
-    wavefront(give_back(1, second), CHUNKS)
+    listed(dispatch(0, first), CHUNKS, 2 * dk)
+    listed(give_back(0, first) + dispatch(1, second), CHUNKS, 2 * dk)
+    listed(give_back(1, second), CHUNKS, 2 * dk)
     for one in sent:
         one.wait_send()
 
@@ -303,6 +338,7 @@
             pltpu.VMEM((total, hdev), F32),
             pltpu.VMEM((total, 2 * hdev), F32),
             pltpu.VMEM((total, 2 * hdev), BF16),
+            pltpu.VMEM((2, tok, 1), F32),
             pltpu.VMEM((2, tok, experts * cp), BF16),
             pltpu.VMEM((rows, experts * cp), BF16),
             pltpu.VMEM(steps + (experts * cp, dk), BF16),
@@ -328,7 +364,8 @@
             collective_id=0, has_side_effects=True, vmem_limit_bytes=56 * 1024 * 1024
         ),
     )(
-        entering[0], routes[:, 0], gates[:, 0], saved[0, 0], w_in[0, 0], w_out[0, 0]
+        entering[0], routes.reshape(2, 1, tok), gates.reshape(2, 1, tok),
+        saved[0, 0], w_in[0, 0], w_out[0, 0],
     )
     return out[:, None]
 

time: 125 us -> 112 us (0.90)
  Pallas kernels: 120 us -> 110 us
  local copies, waits for them, and re-layouts: 4.56 us -> 1.82 us
    pallas_call x1, Pallas kernels: 120 us -> 110 us  [shards(): pl.pallas_call(functools.partial(kernel, experts, cap, cp), out_shape=jax...]
    squeeze x2 -> x0, local copies, waits for them, and re-layouts: 2.75 us -> none  [the longest x1 1.38 us: shards(): routes[:, 0]]
where the time goes in v3:
time: 112 us; the launch traced here: 111 us
  Pallas kernels  110 us (98%)
  local copies, waits for them, and re-layouts  1.82 us (2%)
    pallas_call x1, Pallas kernels, shards(): pl.pallas_call(functools.partial(kernel, experts, cap, cp), out_shape=jax...  110 us

profile of v3, /device:TPU:0, one launch (start us, length us, event | category | flops | bytes accessed | tf_op | source)
XLA Modules:
  0.0 111.4 jit_solution(8543302991000838809)
XLA Ops:
  0.0 109.6 %shard_map.64 = bf16[2,32,3584]{2,1,0:T(8,128)(2,1)} custom-call(bf16[32,3584]{1,0:T(8,128)(2,1)} %bitcast.17, s32[2,1,32]{2,1,0:T(1,128)} %bitcast.18, f32[2,1,32]{2,1,0:T(1,128)} %bitcast.19, bf16[384,384]{1,0:T(8,128)(2,1)} %bitcast.16, bf16[3584,384]{1,0:T(8,128)(2,1)} %bitcast.13, bf16[192,3584]{1,0:T(8,128)(2,1)} %bitcast.15), custom_call_target="tpu_custom_call" | custom-call | tf_op jit(solution)/shard_map/pallas_call | solution.py:328
  109.6 1.8 %copy.11 = bf16[2,1,32,3584]{3,2,1,0:T(8,128)(2,1)} copy(bf16[2,1,32,3584]{3,2,1,0:T(8,128)(2,1)} %bitcast.14) | data formatting | bytes 917504

commit v4 on v3

--- a/solution.py
+++ b/solution.py
@@ -60,7 +60,7 @@
 
 
 def kernel(
-    experts, cap, cp, entering, routes, gates, saved_hbm, w_in_hbm, w_out_hbm, out,
+    experts, cap, fold, cp, entering, routes, gates, saved_hbm, w_in_hbm, w_out_hbm, out,
     w_in, w_out, saved, silu_g, slope_u, acc, act, weight, place, merge,
     gbuf, rbuf, agbuf, pbuf, sibbuf, qbuf, rsbuf, ubuf, vbuf, xbuf,
     load_sem, cross_s, cross_r, ag_s, ag_r, fw_s, fw_r, sib_s, sib_r,
@@ -116,12 +116,14 @@
         onehot = (route == iota((tok, 128), 1)).astype(F32)
         before = nn(earlier, onehot.astype(BF16))
         slot = jnp.sum(before * onehot, axis=1, keepdims=True).astype(jnp.int32)
-        target = route * cp + slot
-        place[tick] = (target == iota((tok, experts * cp), 1)).astype(F32).astype(BF16)
+        for h in range(fold):
+            target = route * cp + h * cap + slot
+            spots = target == iota((tok, experts * cp), 1)
+            place[tick, h] = spots.astype(F32).astype(BF16)
     r = iota((rows, experts * cp), 0)
-    merge[...] = (
-        (r // cap * cp + r % cap == iota((rows, experts * cp), 1)).astype(F32).astype(BF16)
-    )
+    for h in range(fold):
+        spots = r // cap * cp + h * cap + r % cap == iota((rows, experts * cp), 1)
+        merge[h] = spots.astype(F32).astype(BF16)
 
     pl.semaphore_wait(barrier, len(greeted))
 
@@ -149,6 +151,15 @@
 
     def tokens(t, k):
         return entering[:, cols(k)] if t == 0 else xbuf[k]
+
+    def part_of(h):
+        return slice(h * dk // fold, (h + 1) * dk // fold)
+
+    def folded(tables, data):
+        total = tn(tables[0], data[:, part_of(0)])
+        for h in range(1, fold):
+            total = total + tn(tables[h], data[:, part_of(h)])
+        return total.astype(BF16)
 
     def prepare_saved():
         loads[0].wait()
@@ -167,7 +178,7 @@
         def spread(k):
             if t == 1:
                 arrive(xbuf.at[k], x_s.at[k], x_r.at[k], partner)
-            gbuf[t, k] = tn(place[t], tokens(t, k)).astype(BF16)
+            gbuf[t, k] = folded(place[t], tokens(t, k))
             for o in range(1, experts):
                 send(
                     gbuf.at[t, k, ds(lax.rem(e + o, experts), cp)],
@@ -185,7 +196,8 @@
                     cross_s.at[t, k, o], cross_r.at[t, k, o], at_expert(o),
                 )
             mine = ds(c * CHIPS + q, rows)
-            agbuf[t, k, mine] = nn(merge[...], rbuf[t, k]).astype(BF16)
+            for h in range(fold):
+                agbuf[t, k, mine, part_of(h)] = nn(merge[h], rbuf[t, k]).astype(BF16)
             for o in range(1, CHIPS):
                 send(
                     agbuf.at[t, k, mine], agbuf.at[t, k, mine],
@@ -223,7 +235,7 @@
                 activate(forward)
 
         return [
-            (spread, 1.0, [("z", cp), ("mid", 2 * cp)]),
+            (spread, 1.0, [("z", cp // fold), ("mid", 2 * cp // fold)]),
             (gather, 1.0, [("y", 2 * rows), ("z", 2 * rows)]),
             (forward_on, 0.0, [("core", half)]),
             (multiply, 4.0, []),
@@ -271,7 +283,7 @@
             for o in range(1, CHIPS):
                 arrive(rsbuf.at[t, k, o], rs_s.at[t, k, o], rs_r.at[t, k, o], at_chip(o))
                 total = total + rsbuf[t, k, o].astype(F32)
-            ubuf[t, k] = tn(merge[...], total.astype(BF16)).astype(BF16)
+            ubuf[t, k] = folded(merge[...], total.astype(BF16))
             for o in range(1, experts):
                 send(
                     ubuf.at[t, k, ds(lax.rem(e + o, experts), cp)],
@@ -286,7 +298,7 @@
                     vbuf.at[t, k, ds(lax.rem(e + experts - o, experts), cp)],
                     ret_s.at[t, k, o], ret_r.at[t, k, o], at_expert(o),
                 )
-            picked = nn(place[t], vbuf[t, k])
+            picked = jnp.concatenate([nn(place[t, h], vbuf[t, k]) for h in range(fold)], axis=1)
             result = (tokens(t, k).astype(F32) + weight[t] * picked).astype(BF16)
             out[t, :, cols(k)] = result
             if t == 0:
@@ -296,7 +308,7 @@
         return [
             (part, 4.0, [("core", half)]),
             (scatter, 1.5, [("y", 2 * rows), ("z", 2 * rows)]),
-            (return_on, 1.0, [("z", cp), ("mid", 2 * cp)]),
+            (return_on, 1.0, [("z", cp // fold), ("mid", 2 * cp // fold)]),
             (combine, 0.7, [("x", tok)]),
         ]
 
@@ -315,7 +327,8 @@
     top = routes.shape[3]
     assert top == 1
     cap = min(tok, max(2, (3 * tok * top + 2 * experts - 1) // (2 * experts)))
-    cp = -(-cap // 16) * 16
+    fold = 2 if cap % 16 and 2 * cap % 16 == 0 else 1
+    cp = -(-fold * cap // 16) * 16
     rows = experts * cap
     total = SHARDS * rows
     half = CHIPS * rows
@@ -326,7 +339,7 @@
     vmem = pl.BlockSpec(memory_space=pltpu.VMEM)
     hbm = pl.BlockSpec(memory_space=pl.ANY)
     out = pl.pallas_call(
-        functools.partial(kernel, experts, cap, cp),
+        functools.partial(kernel, experts, cap, fold, cp),
         out_shape=jax.ShapeDtypeStruct((2, tok, width), BF16),
         in_specs=[vmem] * 3 + [hbm] * 3,
         out_specs=vmem,
@@ -339,17 +352,17 @@
             pltpu.VMEM((total, 2 * hdev), F32),
             pltpu.VMEM((total, 2 * hdev), BF16),
             pltpu.VMEM((2, tok, 1), F32),
-            pltpu.VMEM((2, tok, experts * cp), BF16),
-            pltpu.VMEM((rows, experts * cp), BF16),
-            pltpu.VMEM(steps + (experts * cp, dk), BF16),
-            pltpu.VMEM(steps + (experts * cp, dk), BF16),
+            pltpu.VMEM((2, fold, tok, experts * cp), BF16),
+            pltpu.VMEM((fold, rows, experts * cp), BF16),
+            pltpu.VMEM(steps + (experts * cp, dk // fold), BF16),
+            pltpu.VMEM(steps + (experts * cp, dk // fold), BF16),
             pltpu.VMEM(steps + (total, dk), BF16),
             pltpu.VMEM(steps + (total, dk), BF16),
             pltpu.VMEM(steps + (half, dk), BF16),
             pltpu.VMEM(steps + (half, dk), BF16),
             pltpu.VMEM(steps + (CHIPS, rows, dk), BF16),
-            pltpu.VMEM(steps + (experts * cp, dk), BF16),
-            pltpu.VMEM(steps + (experts * cp, dk), BF16),
+            pltpu.VMEM(steps + (experts * cp, dk // fold), BF16),
+            pltpu.VMEM(steps + (experts * cp, dk // fold), BF16),
             pltpu.VMEM(steps + (tok, dk), BF16),
             dma((3,)),
             dma(steps + (experts,)), dma(steps + (experts,)),

time: 112 us -> 105 us (0.938)
  Pallas kernels: 110 us -> 103 us
    pallas_call x1, Pallas kernels: 110 us -> 103 us  [shards(): pl.pallas_call(functools.partial(kernel, experts, cap, fold, cp), out_sha...]
where the time goes in v4:
time: 105 us; the launch traced here: 104 us
  Pallas kernels  103 us (98%)
  local copies, waits for them, and re-layouts  1.82 us (2%)
    pallas_call x1, Pallas kernels, shards(): pl.pallas_call(functools.partial(kernel, experts, cap, fold, cp), out_sha...  103 us

profile of v4, /device:TPU:0, one launch (start us, length us, event | category | flops | bytes accessed | tf_op | source)
XLA Modules:
  0.0 104.4 jit_solution(3397403905127182454)
XLA Ops:
  0.0 102.6 %shard_map.64 = bf16[2,32,3584]{2,1,0:T(8,128)(2,1)} custom-call(bf16[32,3584]{1,0:T(8,128)(2,1)} %bitcast.17, s32[2,1,32]{2,1,0:T(1,128)} %bitcast.18, f32[2,1,32]{2,1,0:T(1,128)} %bitcast.19, bf16[384,384]{1,0:T(8,128)(2,1)} %bitcast.16, bf16[3584,384]{1,0:T(8,128)(2,1)} %bitcast.13, bf16[192,3584]{1,0:T(8,128)(2,1)} %bitcast.15), custom_call_target="tpu_custom_call" | custom-call | tf_op jit(solution)/shard_map/pallas_call | solution.py:341
  102.6 1.8 %copy.11 = bf16[2,1,32,3584]{3,2,1,0:T(8,128)(2,1)} copy(bf16[2,1,32,3584]{3,2,1,0:T(8,128)(2,1)} %bitcast.14) | data formatting | bytes 917504

commit v5 on v4

--- a/solution.py
+++ b/solution.py
@@ -83,6 +83,8 @@
     def at_chip(o):
         return (sec, e * SHARDS + lax.rem(q + o, CHIPS) * 2 + c)
 
+    y = lax.rem(q, 2)
+    over = {1: 1 + 2 * y, 2: 2, 3: 3 - 2 * y}
     sibling = (sec, me + 1 - 2 * c)
     partner = (sec + 1 - 2 * parity, me)
 
@@ -198,18 +200,27 @@
             mine = ds(c * CHIPS + q, rows)
             for h in range(fold):
                 agbuf[t, k, mine, part_of(h)] = nn(merge[h], rbuf[t, k]).astype(BF16)
-            for o in range(1, CHIPS):
-                send(
-                    agbuf.at[t, k, mine], agbuf.at[t, k, mine],
-                    ag_s.at[t, k, o], ag_r.at[t, k, o], at_chip(o),
-                )
+            for i in (1, 2) if k % 2 else (1, 2, 3):
+                spread_to(k, i, mine)
+
+        def spread_to(k, i, block, to=None):
+            send(
+                agbuf.at[t, k, block], agbuf.at[t, k, block],
+                ag_s.at[t, k, i], ag_r.at[t, k, i], at_chip(over[to or i]),
+            )
+
+        def landed(k, i):
+            block = ds(c * CHIPS + lax.rem(q + over[i], CHIPS), rows)
+            arrive(agbuf.at[t, k, block], ag_s.at[t, k, i], ag_r.at[t, k, i], at_chip(over[i]))
+            return block
+
+        def pass_on(k):
+            if k % 2:
+                spread_to(k, 3, landed(k, 2), to=1)
 
         def forward_on(k):
-            for o in range(1, CHIPS):
-                arrive(
-                    agbuf.at[t, k, ds(c * CHIPS + lax.rem(q + CHIPS - o, CHIPS), rows)],
-                    ag_s.at[t, k, o], ag_r.at[t, k, o], at_chip(o),
-                )
+            for i in (1, 3) if k % 2 else (1, 2, 3):
+                landed(k, i)
             send(
                 agbuf.at[t, k, ds(c, half)], agbuf.at[t, k, ds(c, half)],
                 fw_s.at[t, k], fw_r.at[t, k], sibling,
@@ -236,7 +247,8 @@
 
         return [
             (spread, 1.0, [("z", cp // fold), ("mid", 2 * cp // fold)]),
-            (gather, 1.0, [("y", 2 * rows), ("z", 2 * rows)]),
+            (gather, 1.0, [("y", 3 * rows // 2), ("z", 3 * rows // 2)]),
+            (pass_on, 0.0, [("y", rows // 2)]),
             (forward_on, 0.0, [("core", half)]),
             (multiply, 4.0, []),
         ]

time: 105 us -> 105 us (level)
  no operation moved by 1% of the time
where the time goes in v5:
time: 105 us
  Pallas kernels  103 us (98%)
  local copies, waits for them, and re-layouts  1.82 us (2%)
    pallas_call x1, Pallas kernels, shards(): pl.pallas_call(functools.partial(kernel, experts, cap, fold, cp), out_sha...  103 us

profile of v5, /device:TPU:0, one launch (start us, length us, event | category | flops | bytes accessed | tf_op | source)
XLA Modules:
  0.0 104.8 jit_solution(16674043766647864915)
XLA Ops:
  0.0 103.0 %shard_map.64 = bf16[2,32,3584]{2,1,0:T(8,128)(2,1)} custom-call(bf16[32,3584]{1,0:T(8,128)(2,1)} %bitcast.17, s32[2,1,32]{2,1,0:T(1,128)} %bitcast.18, f32[2,1,32]{2,1,0:T(1,128)} %bitcast.19, bf16[384,384]{1,0:T(8,128)(2,1)} %bitcast.16, bf16[3584,384]{1,0:T(8,128)(2,1)} %bitcast.13, bf16[192,3584]{1,0:T(8,128)(2,1)} %bitcast.15), custom_call_target="tpu_custom_call" | custom-call | tf_op jit(solution)/shard_map/pallas_call | solution.py:353
  103.0 1.8 %copy.11 = bf16[2,1,32,3584]{3,2,1,0:T(8,128)(2,1)} copy(bf16[2,1,32,3584]{3,2,1,0:T(8,128)(2,1)} %bitcast.14) | data formatting | bytes 917504

commit v6 on v5

--- a/solution.py
+++ b/solution.py
@@ -127,8 +127,6 @@
         spots = r // cap * cp + h * cap + r % cap == iota((rows, experts * cp), 1)
         merge[h] = spots.astype(F32).astype(BF16)
 
-    pl.semaphore_wait(barrier, len(greeted))
-
     def copy(src, dst, send, recv, device):
         return pltpu.make_async_remote_copy(
             src_ref=src, dst_ref=dst, send_sem=send, recv_sem=recv,
@@ -188,8 +186,6 @@
                     cross_s.at[t, k, o], cross_r.at[t, k, o], at_expert(o),
                 )
             rbuf[t, k, ds(e, cp)] = gbuf[t, k, ds(e, cp)]
-            if t == 0 and k == 2:
-                prepare_saved()
 
         def gather(k):
             for o in range(1, experts):
@@ -324,6 +320,8 @@
             (combine, 0.7, [("x", tok)]),
         ]
 
+    prepare_saved()
+    pl.semaphore_wait(barrier, len(greeted))
     stage_x, xbuf = xbuf.at[0], xbuf.at[1]
     first, second = parity == 0, parity == 1
     listed(dispatch(0, first), CHUNKS, 2 * dk)

time: 105 us -> 107 us (1.019)
  Pallas kernels: 103 us -> 105 us
    pallas_call x1, Pallas kernels: 103 us -> 105 us  [shards(): pl.pallas_call(functools.partial(kernel, experts, cap, fold, cp), out_sha...]
where the time goes in v6:
time: 107 us; the launch traced here: 106 us
  Pallas kernels  105 us (98%)
  local copies, waits for them, and re-layouts  1.82 us (2%)
    pallas_call x1, Pallas kernels, shards(): pl.pallas_call(functools.partial(kernel, experts, cap, fold, cp), out_sha...  105 us

profile of v6, /device:TPU:0, one launch (start us, length us, event | category | flops | bytes accessed | tf_op | source)
XLA Modules:
  0.0 106.5 jit_solution(10873163809921402188)
XLA Ops:
  0.0 104.6 %shard_map.64 = bf16[2,32,3584]{2,1,0:T(8,128)(2,1)} custom-call(bf16[32,3584]{1,0:T(8,128)(2,1)} %bitcast.17, s32[2,1,32]{2,1,0:T(1,128)} %bitcast.18, f32[2,1,32]{2,1,0:T(1,128)} %bitcast.19, bf16[384,384]{1,0:T(8,128)(2,1)} %bitcast.16, bf16[3584,384]{1,0:T(8,128)(2,1)} %bitcast.13, bf16[192,3584]{1,0:T(8,128)(2,1)} %bitcast.15), custom_call_target="tpu_custom_call" | custom-call | tf_op jit(solution)/shard_map/pallas_call | solution.py:351
  104.7 1.8 %copy.11 = bf16[2,1,32,3584]{3,2,1,0:T(8,128)(2,1)} copy(bf16[2,1,32,3584]{3,2,1,0:T(8,128)(2,1)} %bitcast.14) | data formatting | bytes 917504
